TPU v7x, 32 devices: a whole 2x2x4 slice. The times are simulated.
32 devices in a mesh: leaf: 8 (over z, x), vec: 4 (over y, core).
Axes of the slice: x: 2, y: 2, z: 4, core: 2. Of those that a mesh axis runs over, the one named last changes fastest.
Arguments:
- vectors: bfloat16 [16384, 512], P('leaf', 'vec'), may hold values from -6 to 6
- leaf_basis: bfloat16 [32, 512, 256], P('leaf'), may hold values from -0.25 to 0.25
- up_leaf: bfloat16 [32, 256, 256], P('leaf'), may hold values from -0.25 to 0.25
- up_mid: bfloat16 [16, 256, 256], P('leaf'), may hold values from -0.25 to 0.25
- top_up: bfloat16 [8, 256, 256], P('leaf'), may hold values from -0.125 to 0.125
- top_down: bfloat16 [8, 256, 256], P('leaf'), may hold values from -0.375 to 0.375
- couplings: bfloat16 [16, 256, 256], replicated, may hold values from -0.125 to 0.125
- coupling_top: bfloat16 [256, 256], replicated, may hold values from -0.375 to 0.375
- near_blocks: bfloat16 [32, 5, 512, 512], P('leaf', None, 'vec'), may hold values from -0.125 to 0.125
- far_owner: int32 [448, 1], replicated, may hold values from 0 to 7; in each aligned block of 56 rows (0 to 55, 56 to 111, ...) at most 9 rows name the same one
- far_pick: int32 [448], replicated, may hold values from 0 to 3
- far_kind: int32 [448], P('leaf'), may hold values from 0 to 15
Outputs:
- result: bfloat16 [16384, 512], P('leaf', 'vec')
Inputs may be any that keep to these rules, and one draw needn't show every extreme that they name: `far_owner`: among the 56 rows r of one aligned block (the far pairs of one subtree), no subtree is named more than 9 times, and in every draw some block names some subtree exactly 9 times.
All inputs are finite; a program needn't handle non-finite values.
Results may differ from a plain program's by a relative error of at most 0.009.
Values may be sent and summed in bfloat16 or wider, within the bound.
A program may use at most 128 MiB of HBM per device.

v0:
```python
import jax
import jax.numpy as jnp
import numpy as np
from jax import lax
from jax.sharding import PartitionSpec as P

LEAF = 512
RANK = 256
NEAR = 5
FAR_LEAF = 8
FAR_MID = 8
FAR_ROOT = 8


def with_halo(block, sides, width):
    for axis, dim in sides:
        count = lax.axis_size(axis)
        forward = [(i, i + 1) for i in range(count - 1)]
        backward = [(target, source) for source, target in forward]
        low = lax.ppermute(
            lax.slice_in_dim(block, block.shape[dim] - width, None, axis=dim), axis, forward
        )
        high = lax.ppermute(lax.slice_in_dim(block, 0, width, axis=dim), axis, backward)
        block = jnp.concatenate([low, block, high], axis=dim)
    return block


def node_table():
    node_bases = np.concatenate(
        [np.zeros(4 * FAR_LEAF), np.full(2 * FAR_MID, 4), np.full(FAR_ROOT, 6)]
    ).astype(np.int32)
    moduli = np.concatenate(
        [np.full(4 * FAR_LEAF, 4), np.full(2 * FAR_MID, 2), np.full(FAR_ROOT, 1)]
    ).astype(np.int32)
    return (jnp.asarray(node_bases), jnp.asarray(moduli))


def body(
    vectors,
    leaf_basis,
    up_leaf,
    up_mid,
    top_up,
    top_down,
    couplings,
    coupling_top,
    near_blocks,
    far_owner,
    far_pick,
    far_kind,
):
    leaf_count = lax.axis_size("leaf")
    device = lax.axis_index("leaf")
    vec_width = vectors.shape[1]
    local_leaves = leaf_basis.shape[0]
    span_rows = local_leaves * LEAF
    blocked = vectors.reshape(local_leaves, LEAF, vec_width)
    coeff_leaf = jnp.einsum(
        "nlr,nlv->nrv", leaf_basis, blocked, preferred_element_type=jnp.float32
    ).astype(jnp.bfloat16)
    coeff_mid = (
        jnp.einsum("nrs,nrv->nsv", up_leaf, coeff_leaf, preferred_element_type=jnp.float32)
        .reshape(local_leaves // 2, 2, RANK, vec_width)
        .sum(axis=1)
        .astype(jnp.bfloat16)
    )
    coeff_root = (
        jnp.einsum("nrs,nrv->nsv", up_mid, coeff_mid, preferred_element_type=jnp.float32)
        .reshape(1, 2, RANK, vec_width)
        .sum(axis=1)
        .astype(jnp.bfloat16)
    )
    top_term = jnp.einsum("nrs,nrv->sv", top_up, coeff_root, preferred_element_type=jnp.float32)
    top_coeff = lax.psum(top_term, "leaf").astype(jnp.bfloat16)
    top_local = jnp.dot(coupling_top, top_coeff, preferred_element_type=jnp.float32).astype(
        jnp.bfloat16
    )
    top_share = jnp.einsum("nrs,sv->nrv", top_down, top_local, preferred_element_type=jnp.float32)
    all_coeffs = jnp.concatenate([coeff_leaf, coeff_mid, coeff_root], axis=0)
    node_bases, moduli = node_table()
    far_rows = far_kind.shape[0]
    owners = far_owner.reshape(leaf_count, far_rows)
    node_ids = node_bases[None, :] + far_pick.reshape(leaf_count, far_rows) % moduli[None, :]
    own_owner = lax.dynamic_index_in_dim(owners, device, 0, keepdims=False)
    own_nodes = lax.dynamic_index_in_dim(node_ids, device, 0, keepdims=False)
    gathered = lax.all_gather(all_coeffs, "leaf", axis=0, tiled=True)
    partner_coeffs = jnp.take(gathered, own_owner * all_coeffs.shape[0] + own_nodes, axis=0)
    matrices = jnp.take(couplings, far_kind, axis=0)
    products = jnp.einsum(
        "frs,fsv->frv", matrices, partner_coeffs, preferred_element_type=jnp.float32
    )
    first_end = 4 * FAR_LEAF
    second_end = first_end + 2 * FAR_MID
    far_leaf = products[:first_end].reshape(local_leaves, FAR_LEAF, RANK, vec_width).sum(axis=1)
    far_mid = (
        products[first_end:second_end]
        .reshape(local_leaves // 2, FAR_MID, RANK, vec_width)
        .sum(axis=1)
    )
    far_root = products[second_end:].reshape(1, FAR_ROOT, RANK, vec_width).sum(axis=1)
    down_root = (far_root + top_share).astype(jnp.bfloat16)
    down_mid = (
        far_mid
        + jnp.einsum(
            "nrs,nsv->nrv",
            up_mid,
            jnp.repeat(down_root, 2, axis=0),
            preferred_element_type=jnp.float32,
        )
    ).astype(jnp.bfloat16)
    down_leaf = (
        far_leaf
        + jnp.einsum(
            "nrs,nsv->nrv",
            up_leaf,
            jnp.repeat(down_mid, 2, axis=0),
            preferred_element_type=jnp.float32,
        )
    ).astype(jnp.bfloat16)
    far_field = jnp.einsum(
        "nlr,nrv->nlv", leaf_basis, down_leaf, preferred_element_type=jnp.float32
    )
    widened = with_halo(vectors, (("leaf", 0),), NEAR // 2 * LEAF)
    block_part = lax.all_gather(near_blocks, "vec", axis=2, tiled=True)
    running = jnp.zeros((local_leaves, block_part.shape[2], vec_width), jnp.float32)
    for offset in range(NEAR):
        window = widened[offset * LEAF : offset * LEAF + span_rows].reshape(
            local_leaves, LEAF, vec_width
        )
        running = running + jnp.einsum(
            "nil,nlv->niv", block_part[:, offset], window, preferred_element_type=jnp.float32
        )
    return (far_field + running).reshape(span_rows, vec_width).astype(jnp.bfloat16)


def solution(mesh):
    placed = (
        P("leaf", "vec"),
        P("leaf", None, None),
        P("leaf", None, None),
        P("leaf", None, None),
        P("leaf", None, None),
        P("leaf", None, None),
        P(),
        P(),
        P("leaf", None, "vec", None),
        P(),
        P(),
        P("leaf"),
    )
    return jax.shard_map(
        body, mesh=mesh, in_specs=placed, out_specs=P("leaf", "vec"), check_vma=False
    )
```

profile of v0, /device:TPU:0, one launch (start us, length us, event | category | flops | bytes accessed | tf_op | source)
XLA Modules:
  0.0 182.2 jit_solution(11692577169953854747)
XLA Ops:
  6.5 2.0 %convolution_convert_fusion = bf16[4,256,128]{2,1,0:T(8,128)(2,1)S(1)} fusion(bf16[4,512,256]{2,1,0:T(8,128)(2,1)} %param.15, bf16[4,512,128]{2,1,0:T(8,128)(2,1)} %bitcast.126), kind=kOutput, calls=%fused_computation.34 | convolution fusion | flops 134348800 | bytes 1835008 | tf_op jit(solution)/shard_map/nlr,nlv->nrv/dot_general | solution.py:58
  8.6 1.3 bitcast_reduce_fusion.2
  10.0 1.2 fusion.26
  11.3 0.8 pad_maximum_fusion
  12.2 3.6 %copy.42 = bf16[4,5,128,512]{3,2,0,1:T(8,128)(2,1)} copy(bf16[4,5,128,512]{3,2,1,0:T(8,128)(2,1)} %param.22) | data formatting | bytes 5242880 | tf_op args[8]
  15.9 0.8 fusion.38
  16.7 4.8 %collective-permute-start = (bf16[1024,128]{1,0:T(8,128)(2,1)}, bf16[1024,128]{1,0:T(8,128)(2,1)S(1)}, u32[]{:S(2)}, u32[]{:S(2)}) collective-permute-start(bf16[1024,128]{1,0:T(8,128)(2,1)} %get-tuple-element.13), channel_id=1, source_target_pairs={{0,4},{4,8},{8,12},{12,16},{16,20},{20,24},{24,28},{1,5},{5,9},{9,... | collective-permute-start | bytes 786440 | tf_op jit(solution)/shard_map/ppermute | solution.py:20
  21.6 1.3 collective-permute-start.1
  23.0 0.5 broadcast.66
  23.5 0.6 reduce.8
  24.4 5.3 %gather_fusion = bf16[56,256,256]{2,1,0:T(8,128)(2,1)} fusion(bf16[16,256,256]{2,1,0:T(8,128)(2,1)S(1)} %copy-done, s32[1024]{0:T(1024)S(1)} %pad_clamp_fusion.1), kind=kCustom, calls=%fused_computation | custom fusion | bytes 14680288 | tf_op jit(solution)/shard_map/jit(_take)/gather | solution.py:88
  29.7 42.1 %all-reduce.1 = bf16[256,128]{0,1:T(8,128)(2,1)} all-reduce(f32[256,128]{0,1:T(8,128)S(1)} %convolution_bitcast_fusion.5), channel_id=1, replica_groups=mesh['leaf'=8,'vec'=4] {'leaf'}, use_global_device_ids=true, to_apply=%region_4.5 | all-reduce | flops 32768 | bytes 196608 | tf_op jit(solution)/shard_map/psum | solution.py:74
  72.2 1.1 fusion.37
  73.3 1.0 fusion.36
  74.3 16.7 %all-gather.3.cloned.1.call-done = bf16[56,256,128]{2,1,0:T(8,128)(2,1)} async-done(((bf16[7,256,128]{2,1,0:T(8,128)(2,1)}), bf16[56,256,128]{2,1,0:T(8,128)(2,1)}) %all-gather.3.cloned.1.call-update) | async-done | bytes 3670032 | tf_op jit(solution)/shard_map/all_gather | solution.py:86
  91.0 4.9 %gather_fusion.1 = bf16[56,256,128]{2,1,0:T(8,128)(2,1)} fusion(bf16[56,256,128]{2,1,0:T(8,128)(2,1)} %all-gather.3.cloned.1.call-done, s32[1024]{0:T(1024)S(1)} %pad_clamp_fusion), kind=kCustom, calls=%fused_computation.1 | custom fusion | bytes 7340256 | tf_op jit(solution)/shard_map/jit(_take)/gather | solution.py:87
  95.9 7.5 %fusion = f32[56,256,128]{2,1,0:T(8,128)S(1)} fusion(bf16[56,256,256]{2,1,0:T(8,128)(2,1)} %gather_fusion, pred[56]{0:T(512)(128)(4,1)S(1)} %get-tuple-element.15, bf16[56,256,128]{2,1,0:T(8,128)(2,1)} %gather_fusion.1, pred[56]{0:T(512)(128)(4,1)S(1)} %get-tuple-element.5), kind=kOutput, calls=%fused_computation.2 | convolution fusion | flops 945029120 | bytes 18350192 | tf_op jit(solution)/shard_map/frs,fsv->frv/dot_general | solution.py:89
  103.5 3.0 %copy-done.1 = f32[56,256,128]{2,1,0:T(8,128)} copy-done((f32[56,256,128]{2,1,0:T(8,128)}, f32[56,256,128]{2,1,0:T(8,128)S(1)}, u32[]{:S(2)}) %copy-start.1) | copy-done | bytes 7340056
  106.7 1.7 bitcast_reduce_fusion.1
  108.4 0.8 copy.40
  109.3 2.4 %bitcast_reduce_fusion = f32[4,256,128]{2,1,0:T(8,128)S(1)} fusion(f32[56,256,128]{2,1,0:T(8,128)} %copy-done.1), kind=kLoop, calls=%fused_computation.5 | loop fusion | flops 917504 | bytes 4718592 | tf_op jit(solution)/shard_map/reduce_sum | solution.py:94
  111.7 1.0 copy.41
  112.7 1.3 fusion.27
  114.0 1.2 fusion.24
  115.3 3.2 %convolution_bitcast_fusion = f32[4,512,128]{1,2,0:T(8,128)} fusion(bf16[4,512,256]{2,1,0:T(8,128)(2,1)} %param.15, f32[4,256,128]{1,2,0:T(8,128)} %copy.41, bf16[4,256,128]{1,2,0:T(8,128)(2,1)S(1)} %bitcast.132, bf16[4,256,256]{2,1,0:T(8,128)(2,1)} %param.16), kind=kOutput, calls=%fused_computation.23 | convolution fusion | flops 201588736 | bytes 3407872 | tf_op jit(solution)/shard_map/nlr,nrv->nlv/dot_general | solution.py:120
  118.5 43.4 %all-gather.5.cloned.1.call-done = bf16[4,5,512,512]{3,2,0,1:T(8,128)(2,1)} async-done(((bf16[4,5,128,512]{3,2,0,1:T(8,128)(2,1)}), bf16[4,5,512,512]{3,2,0,1:T(8,128)(2,1)}) %all-gather.5.cloned.1.call-update) | async-done | bytes 10485776 | tf_op jit(solution)/shard_map/all_gather | solution.py:124
  161.9 2.5 %fusion.8 = f32[4,512,128]{1,2,0:T(8,128)S(1)} fusion(bf16[4,512,128]{2,1,0:T(8,128)(2,1)S(1)} %bitcast.127, bf16[4,5,512,512]{3,2,0,1:T(8,128)(2,1)} %all-gather.5.cloned.1.call-done), kind=kOutput, calls=%fused_computation.14 | convolution fusion | flops 268435456 | bytes 3670016 | tf_op jit(solution)/shard_map/nil,nlv->niv/dot_general | solution.py:130
  164.4 2.5 %fusion.9 = f32[4,128,512]{2,1,0:T(8,128)S(1)} fusion(bf16[4,512,128]{2,1,0:T(8,128)(2,1)S(1)} %bitcast.129, bf16[4,5,512,512]{3,2,0,1:T(8,128)(2,1)} %all-gather.5.cloned.1.call-done), kind=kOutput, calls=%fused_computation.16 | convolution fusion | flops 268435456 | bytes 3670016 | tf_op jit(solution)/shard_map/nil,nlv->niv/dot_general | solution.py:130
  166.9 2.4 %fusion.13 = f32[4,512,128]{1,2,0:T(8,128)S(1)} fusion(bf16[4,512,128]{2,1,0:T(8,128)(2,1)S(1)} %bitcast.130, bf16[4,5,512,512]{3,2,0,1:T(8,128)(2,1)} %all-gather.5.cloned.1.call-done), kind=kOutput, calls=%fused_computation.22 | convolution fusion | flops 268435456 | bytes 3670016 | tf_op jit(solution)/shard_map/nil,nlv->niv/dot_general | solution.py:130
  169.3 2.6 %fusion.19 = f32[4,512,128]{1,2,0:T(8,128)S(1)} fusion(f32[4,512,128]{1,2,0:T(8,128)S(1)} %fusion.8, f32[4,128,512]{2,1,0:T(8,128)S(1)} %fusion.9, bf16[4,512,128]{2,1,0:T(8,128)(2,1)S(1)} %bitcast.131, bf16[4,5,512,512]{3,2,0,1:T(8,128)(2,1)} %all-gather.5.cloned.1.call-done), kind=kOutput, calls=%fused_computation.29 | convolution fusion | flops 268959744 | bytes 5767168 | tf_op jit(solution)/shard_map/nil,nlv->niv/dot_general | solution.py:130
  171.9 2.5 %fusion.20 = bf16[4,512,128]{1,2,0:T(8,128)(2,1)S(1)} fusion(f32[4,512,128]{1,2,0:T(8,128)S(1)} %copy-done.3, f32[4,512,128]{1,2,0:T(8,128)S(1)} %fusion.13, f32[4,512,128]{1,2,0:T(8,128)S(1)} %fusion.19, bf16[4,512,128]{2,1,0:T(8,128)(2,1)S(1)} %bitcast.128, bf16[4,5,512,512]{3,2,0,1:T(8,128)(2,1)} %all-gather.5.cloned.1.call-done), kind=kOutput, calls=%fused_computation.30 | convolution fusion | flops 269484032 | bytes 6291456 | tf_op jit(solution)/shard_map/nil,nlv->niv/dot_general | solution.py:130
  174.4 1.0 copy.48
  (51 shorter events, 1.1 us)
Async XLA Ops:
  6.5 17.9 %copy-start = (bf16[16,256,256]{2,1,0:T(8,128)(2,1)S(1)}, bf16[16,256,256]{2,1,0:T(8,128)(2,1)}, u32[]{:S(2)}) copy-start(bf16[16,256,256]{2,1,0:T(8,128)(2,1)} %param.20) | copy-start | bytes 6291460
  6.5 84.5 %all-gather.3.cloned.1.call-start = ((), (), s32[]{:S(2)}) async-start(), calls=%async_computation | async-start | bytes 4128768 | tf_op jit(solution)/shard_map/all_gather | solution.py:86
  12.1 3.8 %copy-start.2 = (bf16[2048,128]{1,0:T(8,128)(2,1)S(1)}, bf16[2048,128]{1,0:T(8,128)(2,1)}, u32[]{:S(2)}) copy-start(bf16[2048,128]{1,0:T(8,128)(2,1)} %param.14) | copy-start | bytes 1572868
  12.1 10.8 %copy-start.10 = (s32[448]{0:T(512)S(1)}, s32[448]{0:T(512)}, u32[]{:S(2)}) copy-start(s32[448]{0:T(512)} %param.24) | copy-start | bytes 5380
  12.1 11.4 %copy-start.11 = (s32[448,1]{0,1:T(1,128)S(1)}, s32[448,1]{0,1:T(1,128)}, u32[]{:S(2)}) copy-start(s32[448,1]{0,1:T(1,128)} %param.23) | copy-start | bytes 5380
  12.2 12.0 %copy-start.9 = (bf16[1,256,256]{2,1,0:T(8,128)(2,1)S(1)}, bf16[1,256,256]{2,1,0:T(8,128)(2,1)}, u32[]{:S(2)}) copy-start(bf16[1,256,256]{2,1,0:T(8,128)(2,1)} %param.18) | copy-start | bytes 393220
  12.2 12.2 %copy-start.12 = (s32[56]{0:T(128)S(1)}, s32[56]{0:T(128)}, u32[]{:S(2)}) copy-start(s32[56]{0:T(128)} %param.25) | copy-start | bytes 676
  12.2 149.7 %all-gather.5.cloned.1.call-start = ((), (), s32[]{:S(2)}) async-start(), calls=%async_computation.1 | async-start | bytes 13107200 | tf_op jit(solution)/shard_map/all_gather | solution.py:124
  16.7 55.3 %collective-permute-start = (bf16[1024,128]{1,0:T(8,128)(2,1)}, bf16[1024,128]{1,0:T(8,128)(2,1)S(1)}, u32[]{:S(2)}, u32[]{:S(2)}) collective-permute-start(bf16[1024,128]{1,0:T(8,128)(2,1)} %get-tuple-element.13), channel_id=1, source_target_pairs={{0,4},{4,8},{8,12},{12,16},{16,20},{20,24},{24,28},{1,5},{5,9},{9,... | collective-permute-start | bytes 786440 | tf_op jit(solution)/shard_map/ppermute | solution.py:20
  21.6 50.6 %collective-permute-start.1 = (bf16[1024,128]{1,0:T(8,128)(2,1)}, bf16[1024,128]{1,0:T(8,128)(2,1)S(1)}, u32[]{:S(2)}, u32[]{:S(2)}) collective-permute-start(bf16[1024,128]{1,0:T(8,128)(2,1)} %get-tuple-element.14), channel_id=1, source_target_pairs={{4,0},{8,4},{12,8},{16,12},{20,16},{24,20},{28,24},{5,1},{9,5},{13... | collective-permute-start | bytes 786440 | tf_op jit(solution)/shard_map/ppermute | solution.py:23
  24.4 47.4 %copy-start.13 = (s32[56]{0:T(128)S(1)}, s32[56]{0:T(128)}, u32[]{:S(2)}) copy-start(s32[56]{0:T(128)} %constant.58.clone) | copy-start | bytes 676
  24.4 47.4 %copy-start.14 = (s32[56]{0:T(128)S(1)}, s32[56]{0:T(128)}, u32[]{:S(2)}) copy-start(s32[56]{0:T(128)} %constant.67) | copy-start | bytes 676
  103.5 3.1 %copy-start.1 = (f32[56,256,128]{2,1,0:T(8,128)}, f32[56,256,128]{2,1,0:T(8,128)S(1)}, u32[]{:S(2)}) copy-start(f32[56,256,128]{2,1,0:T(8,128)S(1)} %fusion) | copy-start | bytes 22020100
  108.4 5.6 %copy-start.8 = (bf16[2,256,256]{2,1,0:T(8,128)(2,1)S(1)}, bf16[2,256,256]{2,1,0:T(8,128)(2,1)}, u32[]{:S(2)}) copy-start(bf16[2,256,256]{2,1,0:T(8,128)(2,1)} %param.17) | copy-start | bytes 786436
  115.2 49.1 %copy-start.5 = (bf16[2048,128]{1,0:T(8,128)(2,1)S(1)}, bf16[2048,128]{1,0:T(8,128)(2,1)}, u32[]{:S(2)}) copy-start(bf16[2048,128]{1,0:T(8,128)(2,1)} %get-tuple-element.10) | copy-start | bytes 1572868
  161.9 5.0 %copy-start.6 = (bf16[2048,128]{1,0:T(8,128)(2,1)S(1)}, bf16[2048,128]{1,0:T(8,128)(2,1)}, u32[]{:S(2)}) copy-start(bf16[2048,128]{1,0:T(8,128)(2,1)} %get-tuple-element.8) | copy-start | bytes 1572868
  164.4 4.9 %copy-start.7 = (bf16[2048,128]{1,0:T(8,128)(2,1)S(1)}, bf16[2048,128]{1,0:T(8,128)(2,1)}, u32[]{:S(2)}) copy-start(bf16[2048,128]{1,0:T(8,128)(2,1)} %get-tuple-element.9) | copy-start | bytes 1572868
  169.3 2.6 %copy-start.3 = (f32[4,512,128]{1,2,0:T(8,128)S(1)}, f32[4,512,128]{1,2,0:T(8,128)}, u32[]{:S(2)}) copy-start(f32[4,512,128]{1,2,0:T(8,128)} %convolution_bitcast_fusion) | copy-start | bytes 3145732
  169.3 2.6 %copy-start.4 = (bf16[2048,128]{1,0:T(8,128)(2,1)S(1)}, bf16[2048,128]{1,0:T(8,128)(2,1)}, u32[]{:S(2)}) copy-start(bf16[2048,128]{1,0:T(8,128)(2,1)} %get-tuple-element.7) | copy-start | bytes 1572868
Sparse Core Ops, SparseCore 0:
  12.2 78.7 all-gather.2
  92.6 69.2 all-gather.4
where the time goes:
time: 183 us; the launch traced here: 182 us
  waiting for transfers between devices  60.1 us (33%)
  blocking collectives  42.1 us (23%)
  matrix products  30.4 us (17%)
  local copies, waits for them, and re-layouts  23.8 us (13%)
  between operations  13.8 us (8%)
  starting transfers between devices  6.18 us (3%)
  other arithmetic  5.81 us (3%)
    all_gather x1, waiting for transfers between devices, body(): block_part = lax.all_gather(near_blocks, 'vec', axis=2, tiled=True)  43.4 us
    psum x1, blocking collectives, body(): top_coeff = lax.psum(top_term, 'leaf').astype(jnp.bfloat16)  42.1 us
    all_gather x1, waiting for transfers between devices, body(): gathered = lax.all_gather(all_coeffs, 'leaf', axis=0, tiled=True)  16.7 us
    dot_general x5, matrix products, body(): jnp.einsum('nil,nlv->niv', block_part[:, offset], window, preferred_eleme...  12.4 us
    dot_general x1, matrix products, body(): jnp.einsum('frs,fsv->frv', matrices, partner_coeffs, preferred_element_ty...  7.52 us
    unnamed x33, local copies, waits for them, and re-layouts  7.3 us
    gather x1, local copies, waits for them, and re-layouts, body(): matrices = jnp.take(couplings, far_kind, axis=0)  5.29 us
    gather x1, local copies, waits for them, and re-layouts, body(): jnp.take(gathered, own_owner * all_coeffs.shape[0] + own_nodes, axis=0)  4.92 us
  transfers between devices with their start and end apart: 4, of which 2 were waited for; matrix products, arithmetic and copies ran while one was open for 21% of the time, Pallas kernels for 0%

commit v1 on v0

v1 whole, which is shorter than its diff:
```python
import functools
import jax
import jax.numpy as jnp
import numpy as np
from jax import lax
from jax.experimental import pallas as pl
from jax.experimental.pallas import tpu as pltpu
from jax.sharding import PartitionSpec as P

LEAF = 512
RANK = 256
NEAR = 5
FAR_LEAF = 8
FAR_MID = 8
FAR_ROOT = 8
HALO = NEAR // 2
CHUNK = 4
F32 = jnp.float32
BF16 = jnp.bfloat16


def dot(a, b):
    return jnp.dot(a, b, preferred_element_type=F32)


def dot_t(a, b):
    return lax.dot_general(a, b, (((0,), (0,)), ((), ())), preferred_element_type=F32)


def ring_position(leaf, count):
    return jnp.where(leaf % 2 == 1, leaf // 2, count - 1 - leaf // 2)


def leaf_at(position, count):
    half = count // 2
    return jnp.where(position < half, 2 * position + 1, 2 * (count - 1 - position))


def kernel(
    n,
    w,
    slot_ref,
    kind_ref,
    vec_hbm,
    basis_hbm,
    up_leaf_hbm,
    up_mid_hbm,
    top_up_hbm,
    top_down_hbm,
    coup_hbm,
    coup_top_hbm,
    near_hbm,
    out_ref,
    vecs,
    basis,
    up_leaf,
    up_mid,
    top_up,
    top_down,
    coup,
    coup_top,
    near,
    low_coeffs,
    high_coeffs,
    acc,
    far,
    near_out,
    near_in,
    local_sem,
    halo_send,
    halo_recv,
    vec_send,
    vec_recv,
    ring_send,
    ring_recv,
    back_send,
    back_recv,
):
    span = vec_hbm.shape[0]
    leaves = span // LEAF
    rows = near.shape[2]
    width = vec_hbm.shape[1]
    halo = HALO * LEAF
    me = lax.axis_index("leaf")
    mv = lax.axis_index("vec")
    pos = ring_position(me, n)
    nxt = leaf_at((pos + 1) % n, n)
    prv = leaf_at((pos + n - 1) % n, n)
    core, high = mv % 2, mv // 2
    highs = w // 2
    buddy = high * 2 + 1 - core

    def at(leaf=None, vec=None):
        return (me if leaf is None else leaf, mv if vec is None else vec)

    locals_ = [
        (vec_hbm, vecs.at[mv, pl.ds(halo, span)]),
        (basis_hbm, basis),
        (up_leaf_hbm, up_leaf),
        (up_mid_hbm, up_mid),
        (top_up_hbm, top_up),
        (near_hbm, near),
        (coup_hbm, coup),
        (top_down_hbm, top_down),
        (coup_top_hbm, coup_top),
    ]
    loads = [
        pltpu.make_async_copy(src, dst, local_sem.at[k]) for k, (src, dst) in enumerate(locals_)
    ]
    for load in loads:
        load.start()

    barrier = pltpu.get_barrier_semaphore()

    def greet(device):
        pl.semaphore_signal(barrier, inc=1, device_id=device, device_id_type=pl.DeviceIdType.MESH)

    greet(at(leaf=nxt))
    greet(at(leaf=prv))
    for d in range(1, w):
        greet(at(vec=(mv + d) % w))

    @pl.when(me > 0)
    def _():
        greet(at(leaf=me - 1))

    @pl.when(me < n - 1)
    def _():
        greet(at(leaf=me + 1))

    pl.semaphore_wait(
        barrier, w + 1 + (me > 0).astype(jnp.int32) + (me < n - 1).astype(jnp.int32)
    )

    def remote(src, dst, send, recv, device):
        return pltpu.make_async_remote_copy(
            src_ref=src,
            dst_ref=dst,
            send_sem=send,
            recv_sem=recv,
            device_id=device,
            device_id_type=pl.DeviceIdType.MESH,
        )

    def halo_copy(side):
        if side == 0:
            src = vec_hbm.at[pl.ds(span - halo, halo)]
            dst = vecs.at[mv, pl.ds(0, halo)]
            to = at(leaf=me + 1)
        else:
            src = vec_hbm.at[pl.ds(0, halo)]
            dst = vecs.at[mv, pl.ds(halo + span, halo)]
            to = at(leaf=me - 1)
        return remote(src, dst, halo_send.at[side], halo_recv.at[side], to)

    has = (me > 0, me < n - 1)

    spans = (pl.ds(halo, span), pl.ds(0, halo), pl.ds(halo + span, halo))

    def part(p, v):
        return vecs.at[v, spans[p]]

    def source(p):
        return vec_hbm if p == 0 else part(p, mv)

    def to_buddy(p):
        return remote(source(p), part(p, mv), vec_send.at[p, 0], vec_recv.at[p, 0], at(vec=buddy))

    def across(p, d):
        peer = ((high + d) % highs) * 2 + core
        return remote(source(p), part(p, mv), vec_send.at[p, d], vec_recv.at[p, d], at(vec=peer))

    def arrived(p, d):
        peer = ((high + highs - d) % highs) * 2 + core
        return remote(
            part(p, peer), part(p, peer), vec_send.at[p, d], vec_recv.at[p, d], at(vec=buddy)
        )

    def pass_on(p, d):
        peer = ((high + highs - d) % highs) * 2 + core
        k = highs - 1 + d
        return remote(
            part(p, peer), part(p, peer), vec_send.at[p, k], vec_recv.at[p, k], at(vec=buddy)
        )

    def from_buddy(p, d):
        other = ((high + highs - d) % highs) * 2 + 1 - core
        k = 0 if d == 0 else highs - 1 + d
        return remote(
            part(p, other), part(p, other), vec_send.at[p, k], vec_recv.at[p, k], at(vec=buddy)
        )

    def start_part(p):
        for d in range(1, highs):
            across(p, d).start()
        to_buddy(p).start()

    def forward_part(p):
        for d in range(1, highs):
            arrived(p, d).wait_recv()
            pass_on(p, d).start()

    def end_part(p):
        for d in range(highs):
            from_buddy(p, d).wait_recv()

    def end_part_sends(p):
        to_buddy(p).wait_send()
        for d in range(1, highs):
            across(p, d).wait_send()
            pass_on(p, d).wait_send()

    @pl.when(has[1])
    def _():
        halo_copy(0).start()

    @pl.when(has[0])
    def _():
        halo_copy(1).start()

    start_part(0)

    half = n // 2

    def ring_slot(direction, distance, chunk):
        origin = (pos + n - distance) % n if direction == 0 else (pos + distance) % n
        return (low_coeffs, high_coeffs)[chunk].at[pl.ds(origin * CHUNK, CHUNK)]

    def ring(direction, step, chunk, distance):
        ref = ring_slot(direction, distance, chunk)
        return remote(
            ref,
            ref,
            ring_send.at[direction, step - 1, chunk],
            ring_recv.at[direction, step - 1, chunk],
            at(leaf=nxt if direction == 0 else prv),
        )

    def has_step(direction, step, chunk):
        return 1 <= step < half or (step == half and chunk == direction)

    def ring_start(step, chunk):
        for direction in range(2):
            if has_step(direction, step, chunk):
                ring(direction, step, chunk, step - 1).start()

    def ring_turn(step, chunk):
        for direction in range(2):
            if has_step(direction, step, chunk):
                ring(direction, step, chunk, step).wait_recv()
                if has_step(direction, step + 1, chunk):
                    ring(direction, step + 1, chunk, step).start()

    base = pos * CHUNK
    loads[0].wait()
    loads[1].wait()
    leaf_coeff = []
    for i in range(leaves):
        c = dot_t(basis[i], vecs[mv, pl.ds(halo + i * LEAF, LEAF)]).astype(BF16)
        low_coeffs[base + i] = c
        leaf_coeff.append(c)
    ring_start(1, 0)
    loads[2].wait()
    loads[3].wait()
    loads[4].wait()
    mids = []
    for m in range(leaves // 2):
        c = (
            dot_t(up_leaf[2 * m], leaf_coeff[2 * m])
            + dot_t(up_leaf[2 * m + 1], leaf_coeff[2 * m + 1])
        ).astype(BF16)
        high_coeffs[base + m] = c
        mids.append(c)
    root = (dot_t(up_mid[0], mids[0]) + dot_t(up_mid[1], mids[1])).astype(BF16)
    high_coeffs[base + 2] = root
    high_coeffs[base + 3] = dot_t(top_up[0], root).astype(BF16)
    ring_start(1, 1)

    for side in range(2):
        p = side + 1

        @pl.when(has[side])
        def _():
            halo_copy(side).wait_recv()
            start_part(p)

        @pl.when(jnp.logical_not(has[side]))
        def _():
            vecs[:, spans[p]] = jnp.zeros((w, halo, width), BF16)

    forward_part(0)
    if half > 1:
        ring_turn(1, 0)
    end_part(0)

    loads[5].wait()

    def near_slot(j):
        low, top = max(0, j - NEAR + 1), min(leaves - 1, j)
        a = jnp.concatenate([near[i, j - i] for i in range(low, top + 1)], axis=0)
        b = jnp.concatenate([vecs[v, pl.ds(j * LEAF, LEAF)] for v in range(w)], axis=1)
        prod = dot(a, b)
        where = pl.ds(low * rows, (top + 1 - low) * rows)
        acc[where] += prod

    order = list(range(HALO, HALO + leaves)) + list(range(HALO)) + list(
        range(HALO + leaves, 2 * HALO + leaves)
    )
    acc[...] = jnp.zeros(acc.shape, F32)
    for j in order[:leaves]:
        near_slot(j)
    if half > 1:
        ring_turn(1, 1)
    for side in range(2):

        @pl.when(has[side])
        def _():
            forward_part(side + 1)

    if half > 2:
        ring_turn(2, 0)
    for side in range(2):

        @pl.when(has[side])
        def _():
            end_part(side + 1)

    for j in order[leaves:]:
        near_slot(j)
    for v in range(w):
        near_out[v] = acc[:, v * width : (v + 1) * width].astype(BF16)

    def back(d):
        to = (mv + d) % w
        return remote(
            near_out.at[to], near_in.at[mv], back_send.at[d], back_recv.at[d], at(vec=to)
        )

    def back_arrived(d):
        src = (mv + w - d) % w
        return remote(
            near_in.at[src], near_in.at[src], back_send.at[d], back_recv.at[d], at(vec=src)
        )

    for d in range(1, w):
        back(d).start()
    near_in[mv] = near_out[mv]
    if half > 2:
        ring_turn(2, 1)
    for step in range(3, half):
        ring_turn(step, 0)
        ring_turn(step, 1)
    ring_turn(half, 0)
    loads[6].wait()

    def far_sum(held, first, count):
        total = None
        for k in range(count):
            r = first + k
            term = dot(coup[kind_ref[r]], held[slot_ref[r]])
            total = term if total is None else total + term
        return total

    def far_leaf_step(i, _):
        far[i] = far_sum(low_coeffs, i * FAR_LEAF, FAR_LEAF)
        return _

    lax.fori_loop(0, leaves, far_leaf_step, 0)
    ring_turn(half, 1)
    loads[7].wait()
    loads[8].wait()

    def add_top(k, total):
        return total + high_coeffs[k * CHUNK + CHUNK - 1].astype(F32)

    top_coeff = lax.fori_loop(0, n, add_top, jnp.zeros((RANK, width), F32)).astype(BF16)
    top_local = dot(coup_top[...], top_coeff).astype(BF16)
    first_end = leaves * FAR_LEAF
    second_end = first_end + leaves // 2 * FAR_MID
    down_root = (far_sum(high_coeffs, second_end, FAR_ROOT) + dot(top_down[0], top_local)).astype(BF16)
    for d in range(1, w):
        back_arrived(d).wait_recv()
    for m in range(leaves // 2):
        down_mid = (
            far_sum(high_coeffs, first_end + m * FAR_MID, FAR_MID) + dot(up_mid[m], down_root)
        ).astype(BF16)
        for i in (2 * m, 2 * m + 1):
            down_leaf = (far[i] + dot(up_leaf[i], down_mid)).astype(BF16)
            field = dot(basis[i], down_leaf)
            close = jnp.concatenate(
                [near_in[u, pl.ds(i * rows, rows)] for u in range(w)], axis=0
            ).astype(F32)
            out_ref[pl.ds(i * LEAF, LEAF)] = (field + close).astype(BF16)

    end_part_sends(0)

    @pl.when(has[1])
    def _():
        halo_copy(0).wait_send()
        end_part_sends(2)

    @pl.when(has[0])
    def _():
        halo_copy(1).wait_send()
        end_part_sends(1)

    for step in range(1, half + 1):
        for chunk in range(2):
            for direction in range(2):
                if has_step(direction, step, chunk):
                    ring(direction, step, chunk, step - 1).wait_send()
    for d in range(1, w):
        back(d).wait_send()


def node_table(leaves):
    bases = np.concatenate(
        [np.zeros(leaves * FAR_LEAF), np.zeros(leaves // 2 * FAR_MID), np.full(FAR_ROOT, 2)]
    )
    moduli = np.concatenate(
        [np.full(leaves * FAR_LEAF, 4), np.full(leaves // 2 * FAR_MID, 2), np.full(FAR_ROOT, 1)]
    )
    return jnp.asarray(bases.astype(np.int32)), jnp.asarray(moduli.astype(np.int32))


def body(
    n,
    w,
    vectors,
    leaf_basis,
    up_leaf,
    up_mid,
    top_up,
    top_down,
    couplings,
    coupling_top,
    near_blocks,
    far_owner,
    far_pick,
    far_kind,
):
    device = lax.axis_index("leaf")
    span, width = vectors.shape
    leaves = leaf_basis.shape[0]
    rows = near_blocks.shape[2]
    far_rows = far_kind.shape[0]
    bases, moduli = node_table(leaves)
    owner = lax.dynamic_slice_in_dim(far_owner, device * far_rows, far_rows, 0).reshape(far_rows)
    pick = lax.dynamic_slice_in_dim(far_pick, device * far_rows, far_rows, 0)
    slots = ring_position(owner, n) * CHUNK + bases + pick % moduli
    half = n // 2
    highs = w // 2
    smem = pl.BlockSpec(memory_space=pltpu.SMEM)
    anywhere = pl.BlockSpec(memory_space=pl.ANY)
    dma = pltpu.SemaphoreType.DMA
    operands = (
        vectors,
        leaf_basis,
        up_leaf,
        up_mid,
        top_up,
        top_down,
        couplings,
        coupling_top,
        near_blocks,
    )
    return pl.pallas_call(
        functools.partial(kernel, n, w),
        out_shape=jax.ShapeDtypeStruct((span, width), BF16),
        in_specs=[smem, smem] + [anywhere] * len(operands),
        out_specs=pl.BlockSpec(memory_space=pltpu.VMEM),
        scratch_shapes=[
            pltpu.VMEM((w, span + 2 * HALO * LEAF, width), BF16),
            *[pltpu.VMEM(a.shape, BF16) for a in operands[1:]],
            pltpu.VMEM((n * CHUNK, RANK, width), BF16),
            pltpu.VMEM((n * CHUNK, RANK, width), BF16),
            pltpu.VMEM((leaves * rows, w * width), F32),
            pltpu.VMEM((leaves, RANK, width), F32),
            pltpu.VMEM((w, leaves * rows, width), BF16),
            pltpu.VMEM((w, leaves * rows, width), BF16),
            dma((9,)),
            dma((2,)),
            dma((2,)),
            dma((3, 2 * highs - 1)),
            dma((3, 2 * highs - 1)),
            dma((2, half, 2)),
            dma((2, half, 2)),
            dma((w,)),
            dma((w,)),
        ],
        compiler_params=pltpu.CompilerParams(
            collective_id=0, has_side_effects=True, vmem_limit_bytes=60 * 1024 * 1024
        ),
    )(slots, far_kind, *operands)


def solution(mesh):
    placed = (
        P("leaf", "vec"),
        P("leaf", None, None),
        P("leaf", None, None),
        P("leaf", None, None),
        P("leaf", None, None),
        P("leaf", None, None),
        P(),
        P(),
        P("leaf", None, "vec", None),
        P(),
        P(),
        P("leaf"),
    )
    return jax.shard_map(
        functools.partial(body, mesh.shape["leaf"], mesh.shape["vec"]),
        mesh=mesh,
        in_specs=placed,
        out_specs=P("leaf", "vec"),
        check_vma=False,
    )
```

time: 183 us -> 65.4 us (0.36)
  Pallas kernels: 0 us -> 61.9 us
  waiting for transfers between devices: 60.1 us -> 0 us
  blocking collectives: 42.1 us -> 0 us
  matrix products: 30.4 us -> 0 us
  local copies, waits for them, and re-layouts: 23.8 us -> 1.87 us
  between operations: 13.8 us -> 0.01 us
  starting transfers between devices: 6.18 us -> 0 us
  other arithmetic: 5.81 us -> 1.43 us
    pallas_call x0 -> x1, Pallas kernels: none -> 61.9 us  [body(): pl.pallas_call(functools.partial(kernel, n, w), out_shape=jax.ShapeDtypeS...]
    all_gather x2 -> x0, waiting for transfers between devices: 60.1 us -> none  [the longest x1 43.4 us: body(): block_part = lax.all_gather(near_blocks, 'vec', axis=2, tiled=True)]
    psum x1 -> x0, blocking collectives: 42.1 us -> none  [body(): top_coeff = lax.psum(top_term, 'leaf').astype(jnp.bfloat16)]
    dot_general x13 -> x0, matrix products: 30.4 us -> none  [the longest x5 12.4 us: body(): jnp.einsum('nil,nlv->niv', block_part[:, offset], window, preferred_eleme...]
    gather x2 -> x0, local copies, waits for them, and re-layouts: 10.2 us -> none  [the longest x1 5.29 us: body(): matrices = jnp.take(couplings, far_kind, axis=0)]
    ppermute x2 -> x0, starting transfers between devices: 6.14 us -> none  [the longest x1 4.84 us: with_halo(): lax.ppermute(lax.slice_in_dim(block, block.shape[dim] - width, None, axis...]
    unnamed x33 -> x1, local copies, waits for them, and re-layouts: 7.3 us -> 1.87 us
    reduce_sum x3 -> x0, other arithmetic: 4.22 us -> none  [the longest x1 2.45 us: body(): products[:first_end].reshape(local_leaves, FAR_LEAF, RANK, vec_width)]
  transfers between devices with their start and end apart: 4 -> 0, of which waited for: 2 -> 0; matrix products, arithmetic and copies ran while one was open for 21% -> 0% of each run, Pallas kernels for 0% -> 0%
where the time goes in v1:
time: 65.4 us; the launch traced here: 65.2 us
  Pallas kernels  61.9 us (95%)
  local copies, waits for them, and re-layouts  1.87 us (3%)
  other arithmetic  1.43 us (2%)
    pallas_call x1, Pallas kernels, body(): pl.pallas_call(functools.partial(kernel, n, w), out_shape=jax.ShapeDtypeS...  61.9 us
    unnamed x1, local copies, waits for them, and re-layouts  1.87 us
    add x1, other arithmetic, body(): slots = ring_position(owner, n) * CHUNK + bases + pick % moduli  1.43 us

profile of v1, /device:TPU:0, one launch (start us, length us, event | category | flops | bytes accessed | tf_op | source)
XLA Modules:
  0.0 65.2 jit_solution(14649759558028982610)
XLA Ops:
  0.0 1.4 %fusion.slot_ref = s32[56]{0:T(128)} fusion(s32[56]{0:T(128)} %constant.61, s32[448]{0:T(512)} %param.24, s32[]{:T(128)S(6)} %select_n.29, s32[56]{0:T(128)} %constant.52.clone, s32[448,1]{0,1:T(1,128)} %param.23), kind=kLoop, calls=%fused_computation.7 | loop fusion | flops 1736 | bytes 1124 | tf_op jit(solution)/shard_map/add | solution.py:450
  1.4 61.9 %shard_map.136 = bf16[2048,128]{1,0:T(8,128)(2,1)} custom-call(s32[56]{0:T(128)} %fusion.slot_ref, s32[56]{0:T(128)} %kind_ref.1, bf16[2048,128]{1,0:T(8,128)(2,1)} %vec_hbm.1, bf16[4,512,256]{2,1,0:T(8,128)(2,1)} %basis_hbm.1, bf16[4,256,256]{2,1,0:T(8,128)(2,1)} %up_leaf_hbm.1, bf16[2,256,256]{2,1,0:T(8,128)(2,1)} %up_mid_hbm.1, ...), custom_call_target="tpu_custom_call" | custom-call | tf_op jit(solution)/shard_map/pallas_call | solution.py:467
  63.4 1.9 %copy.16 = bf16[2048,128]{1,0:T(8,128)(2,1)} copy(bf16[2048,128]{1,0:T(8,128)(2,1)} %shard_map.136) | data formatting | bytes 1048576

commit v2 on v1

--- a/solution.py
+++ b/solution.py
@@ -14,7 +14,7 @@
 FAR_MID = 8
 FAR_ROOT = 8
 HALO = NEAR // 2
-CHUNK = 4
+CHUNKS = (4, 3)
 F32 = jnp.float32
 BF16 = jnp.bfloat16
 
@@ -66,6 +66,7 @@
     far,
     near_out,
     near_in,
+    top_share,
     local_sem,
     halo_send,
     halo_recv,
@@ -75,6 +76,8 @@
     ring_recv,
     back_send,
     back_recv,
+    top_send,
+    top_recv,
 ):
     span = vec_hbm.shape[0]
     leaves = span // LEAF
@@ -224,7 +227,9 @@
 
     def ring_slot(direction, distance, chunk):
         origin = (pos + n - distance) % n if direction == 0 else (pos + distance) % n
-        return (low_coeffs, high_coeffs)[chunk].at[pl.ds(origin * CHUNK, CHUNK)]
+        return (low_coeffs, high_coeffs)[chunk].at[
+            pl.ds(origin * CHUNKS[chunk], CHUNKS[chunk])
+        ]
 
     def ring(direction, step, chunk, distance):
         ref = ring_slot(direction, distance, chunk)
@@ -251,7 +256,39 @@
                 if has_step(direction, step + 1, chunk):
                     ring(direction, step + 1, chunk, step).start()
 
-    base = pos * CHUNK
+    out, last = me // 2, half - 1
+
+    def top_copy(src, dst, to):
+        return remote(
+            top_share.at[src], top_share.at[dst], top_send.at[dst], top_recv.at[dst], at(leaf=to)
+        )
+
+    def top_pair():
+        return top_share[0].astype(F32) + top_share[1].astype(F32)
+
+    def top_point(t):
+        if t == 0:
+            top_copy(0, 1, me + 1 - 2 * (me % 2)).wait_recv()
+
+        @pl.when(out == t)
+        def _():
+            if t == 0:
+                top_share[4] = jnp.zeros((RANK, width), BF16)
+            else:
+                top_copy(2, 4, me + 2).wait_recv()
+            top_share[2] = (top_pair() + top_share[4].astype(F32)).astype(BF16)
+            top_copy(2, 4, me + 2).start()
+
+        @pl.when(out == last - t)
+        def _():
+            if t == 0:
+                top_share[5] = jnp.zeros((RANK, width), BF16)
+            else:
+                top_copy(3, 5, me - 2).wait_recv()
+            top_share[3] = (top_pair() + top_share[5].astype(F32)).astype(BF16)
+            top_copy(3, 5, me - 2).start()
+
+    base, high_base = pos * CHUNKS[0], pos * CHUNKS[1]
     loads[0].wait()
     loads[1].wait()
     leaf_coeff = []
@@ -269,11 +306,12 @@
             dot_t(up_leaf[2 * m], leaf_coeff[2 * m])
             + dot_t(up_leaf[2 * m + 1], leaf_coeff[2 * m + 1])
         ).astype(BF16)
-        high_coeffs[base + m] = c
+        high_coeffs[high_base + m] = c
         mids.append(c)
     root = (dot_t(up_mid[0], mids[0]) + dot_t(up_mid[1], mids[1])).astype(BF16)
-    high_coeffs[base + 2] = root
-    high_coeffs[base + 3] = dot_t(top_up[0], root).astype(BF16)
+    high_coeffs[high_base + 2] = root
+    top_share[0] = dot_t(top_up[0], root).astype(BF16)
+    top_copy(0, 1, me + 1 - 2 * (me % 2)).start()
     ring_start(1, 1)
 
     for side in range(2):
@@ -291,6 +329,7 @@
     forward_part(0)
     if half > 1:
         ring_turn(1, 0)
+        top_point(0)
     end_part(0)
 
     loads[5].wait()
@@ -311,6 +350,8 @@
         near_slot(j)
     if half > 1:
         ring_turn(1, 1)
+    if last > 1:
+        top_point(1)
     for side in range(2):
 
         @pl.when(has[side])
@@ -347,6 +388,8 @@
     near_in[mv] = near_out[mv]
     if half > 2:
         ring_turn(2, 1)
+    for t in range(2, last):
+        top_point(t)
     for step in range(3, half):
         ring_turn(step, 0)
         ring_turn(step, 1)
@@ -370,10 +413,15 @@
     loads[7].wait()
     loads[8].wait()
 
-    def add_top(k, total):
-        return total + high_coeffs[k * CHUNK + CHUNK - 1].astype(F32)
-
-    top_coeff = lax.fori_loop(0, n, add_top, jnp.zeros((RANK, width), F32)).astype(BF16)
+    @pl.when(out == last)
+    def _():
+        top_copy(2, 4, me - 2).wait_recv()
+
+    @pl.when(out == 0)
+    def _():
+        top_copy(3, 5, me + 2).wait_recv()
+
+    top_coeff = (top_pair() + top_share[4].astype(F32) + top_share[5].astype(F32)).astype(BF16)
     top_local = dot(coup_top[...], top_coeff).astype(BF16)
     first_end = leaves * FAR_LEAF
     second_end = first_end + leaves // 2 * FAR_MID
@@ -411,6 +459,15 @@
                     ring(direction, step, chunk, step - 1).wait_send()
     for d in range(1, w):
         back(d).wait_send()
+    top_copy(0, 1, me + 1 - 2 * (me % 2)).wait_send()
+
+    @pl.when(out < last)
+    def _():
+        top_copy(2, 4, me + 2).wait_send()
+
+    @pl.when(out > 0)
+    def _():
+        top_copy(3, 5, me - 2).wait_send()
 
 
 def node_table(leaves):
@@ -447,7 +504,9 @@
     bases, moduli = node_table(leaves)
     owner = lax.dynamic_slice_in_dim(far_owner, device * far_rows, far_rows, 0).reshape(far_rows)
     pick = lax.dynamic_slice_in_dim(far_pick, device * far_rows, far_rows, 0)
-    slots = ring_position(owner, n) * CHUNK + bases + pick % moduli
+    strides = np.full(far_rows, CHUNKS[1], np.int32)
+    strides[: leaves * FAR_LEAF] = CHUNKS[0]
+    slots = ring_position(owner, n) * strides + bases + pick % moduli
     half = n // 2
     highs = w // 2
     smem = pl.BlockSpec(memory_space=pltpu.SMEM)
@@ -472,12 +531,12 @@
         scratch_shapes=[
             pltpu.VMEM((w, span + 2 * HALO * LEAF, width), BF16),
             *[pltpu.VMEM(a.shape, BF16) for a in operands[1:]],
-            pltpu.VMEM((n * CHUNK, RANK, width), BF16),
-            pltpu.VMEM((n * CHUNK, RANK, width), BF16),
+            *[pltpu.VMEM((n * c, RANK, width), BF16) for c in CHUNKS],
             pltpu.VMEM((leaves * rows, w * width), F32),
             pltpu.VMEM((leaves, RANK, width), F32),
             pltpu.VMEM((w, leaves * rows, width), BF16),
             pltpu.VMEM((w, leaves * rows, width), BF16),
+            pltpu.VMEM((6, RANK, width), BF16),
             dma((9,)),
             dma((2,)),
             dma((2,)),
@@ -487,6 +546,8 @@
             dma((2, half, 2)),
             dma((w,)),
             dma((w,)),
+            dma((6,)),
+            dma((6,)),
         ],
         compiler_params=pltpu.CompilerParams(
             collective_id=0, has_side_effects=True, vmem_limit_bytes=60 * 1024 * 1024

time: 65.4 us -> 62 us (0.948); the launches traced: 65.2 us -> 61 us
  Pallas kernels: 61.9 us -> 57.7 us
    pallas_call x1, Pallas kernels: 61.9 us -> 57.7 us  [body(): pl.pallas_call(functools.partial(kernel, n, w), out_shape=jax.ShapeDtypeS...]
where the time goes in v2:
time: 62 us; the launch traced here: 61 us
  Pallas kernels  57.7 us (93%)
  local copies, waits for them, and re-layouts  1.87 us (3%)
  other arithmetic  1.45 us (2%)
    pallas_call x1, Pallas kernels, body(): pl.pallas_call(functools.partial(kernel, n, w), out_shape=jax.ShapeDtypeS...  57.7 us
    unnamed x1, local copies, waits for them, and re-layouts  1.87 us
    add x1, other arithmetic, body(): slots = ring_position(owner, n) * strides + bases + pick % moduli  1.45 us

profile of v2, /device:TPU:0, one launch (start us, length us, event | category | flops | bytes accessed | tf_op | source)
XLA Modules:
  0.0 61.0 jit_solution(524374129678109513)
XLA Ops:
  0.0 1.4 %fusion.slot_ref = s32[56]{0:T(128)} fusion(s32[56]{0:T(128)} %constant.62, s32[448]{0:T(512)} %param.25, s32[]{:T(128)S(6)} %select_n.29, s32[56]{0:T(128)} %constant.52.clone, s32[56]{0:T(128)} %constant.54.clone, s32[448,1]{0,1:T(1,128)} %param.24), kind=kLoop, calls=%fused_computation.7 | loop fusion | flops 1736 | bytes 1348 | tf_op jit(solution)/shard_map/add | solution.py:509
  1.5 57.7 %shard_map.145 = bf16[2048,128]{1,0:T(8,128)(2,1)} custom-call(s32[56]{0:T(128)} %fusion.slot_ref, s32[56]{0:T(128)} %kind_ref.1, bf16[2048,128]{1,0:T(8,128)(2,1)} %vec_hbm.1, bf16[4,512,256]{2,1,0:T(8,128)(2,1)} %basis_hbm.1, bf16[4,256,256]{2,1,0:T(8,128)(2,1)} %up_leaf_hbm.1, bf16[2,256,256]{2,1,0:T(8,128)(2,1)} %up_mid_hbm.1, ...), custom_call_target="tpu_custom_call" | custom-call | tf_op jit(solution)/shard_map/pallas_call | solution.py:526
  59.1 1.9 %copy.17 = bf16[2048,128]{1,0:T(8,128)(2,1)} copy(bf16[2048,128]{1,0:T(8,128)(2,1)} %shard_map.145) | data formatting | bytes 1048576
